TPU v7x, 32 devices: a whole 2x2x4 slice. The times are simulated.
32 devices in a mesh: dev: 32 (over z, y, x, core).
Axes of the slice: x: 2, y: 2, z: 4, core: 2. Of those that a mesh axis runs over, the one named last changes fastest.
Arguments:
- embeddings: bfloat16 [32768, 768], P('dev')
Outputs:
- keep_weight: float32 [32768], P('dev')
All inputs are finite; a program needn't handle non-finite values.
Results may differ from a plain program's by a relative error of at most 0.0044.
Values may be sent and summed in bfloat16 or wider, within the bound.
A program may use at most 64 MiB of HBM per device.

v0:
```python
import math

import jax
import jax.numpy as jnp
from jax import lax
from jax.sharding import PartitionSpec as P

ROUNDS = 4


sharpness = 10.0


def swapped(value, axis, stride):
    mask = 2**stride
    pairs = [(source, source ^ mask) for source in range(lax.axis_size(axis))]
    return lax.ppermute(value, axis, pairs)


def normalize(values):
    widened = values.astype(jnp.float32)
    scaled = (
        widened
        * lax.rsqrt(jnp.mean(widened * widened, axis=1, keepdims=True) + 1e-06)
        / math.sqrt(values.shape[1])
    )
    return scaled.astype(jnp.bfloat16)


def kernel_tile(left, right):
    similarity = lax.dot_general(
        left, right, (((1,), (1,)), ((), ())), preferred_element_type=jnp.float32
    )
    return jnp.exp(sharpness * (similarity - 1.0))


def fetch_partner(normed, bit_number):
    return swapped(normed, "dev", bit_number)


def shards(embeddings):
    normed = normalize(embeddings)
    player_count = lax.axis_size("dev")
    levels = player_count.bit_length() - 1
    tile_rows = normed.shape[0]
    bit_list = [levels - 1 - round_index for round_index in range(ROUNDS)]
    density = jnp.sum(kernel_tile(normed, normed), axis=1)
    for round_index in range(ROUNDS):
        bit_number = bit_list[round_index]
        partner = fetch_partner(normed, bit_number)
        density = density + jnp.sum(kernel_tile(normed, partner), axis=1)
    weights = 1.0 / density
    total = lax.psum(jnp.sum(weights), "dev")
    return weights * (player_count * tile_rows) / total


def solution(mesh):
    return jax.shard_map(
        shards,
        mesh=mesh,
        in_specs=(P("dev", None),),
        out_specs=P("dev"),
        check_vma=False,
    )
```

profile of v0, /device:TPU:0, one launch (start us, length us, event | category | flops | bytes accessed | tf_op | source)
XLA Modules:
  0.0 121.3 jit_solution(877546836770383698)
XLA Ops:
  0.0 0.0 copy-start
  0.0 1.9 %fusion = f32[1024]{0:T(1024)S(1)} fusion(bf16[1024,768]{1,0:T(8,128)(2,1)} %param.1), kind=kLoop, calls=%fused_computation.7 | loop fusion | flops 2358272 | bytes 1576960 | tf_op jit(solution)/shard_map/reduce_sum | solution.py:24
  1.9 0.0 copy-done
  1.9 0.4 fusion.2
  2.4 3.0 %collective-permute-start.2 = (bf16[1024,768]{1,0:T(8,128)(2,1)S(1)}, bf16[1024,768]{1,0:T(8,128)(2,1)S(1)}, u32[]{:S(2)}, u32[]{:S(2)}) collective-permute-start(bf16[1024,768]{1,0:T(8,128)(2,1)S(1)} %fusion.2), channel_id=1, source_target_pairs={{0,4},{1,5},{2,6},{3,7},{4,0},{5,1},{6,2},{7,3},{8,12},{9,13},{10,... | collective-permute-start | bytes 4718600 | tf_op jit(solution)/shard_map/ppermute | solution.py:17
  5.4 1.6 %collective-permute-start.1 = (bf16[1024,768]{1,0:T(8,128)(2,1)S(1)}, bf16[1024,768]{1,0:T(8,128)(2,1)S(1)}, u32[]{:S(2)}, u32[]{:S(2)}) collective-permute-start(bf16[1024,768]{1,0:T(8,128)(2,1)S(1)} %fusion.2), channel_id=1, source_target_pairs={{0,8},{1,9},{2,10},{3,11},{4,12},{5,13},{6,14},{7,15},{8,0},{9,1},... | collective-permute-start | bytes 4718600 | tf_op jit(solution)/shard_map/ppermute | solution.py:17
  7.0 2.6 %collective-permute-start = (bf16[1024,768]{1,0:T(8,128)(2,1)S(1)}, bf16[1024,768]{1,0:T(8,128)(2,1)S(1)}, u32[]{:S(2)}, u32[]{:S(2)}) collective-permute-start(bf16[1024,768]{1,0:T(8,128)(2,1)S(1)} %fusion.2), channel_id=1, source_target_pairs={{0,16},{1,17},{2,18},{3,19},{4,20},{5,21},{6,22},{7,23},{8,24},{9,... | collective-permute-start | bytes 4718600 | tf_op jit(solution)/shard_map/ppermute | solution.py:17
  9.6 1.5 %collective-permute-start.3 = (bf16[1024,768]{1,0:T(8,128)(2,1)S(1)}, bf16[1024,768]{1,0:T(8,128)(2,1)S(1)}, u32[]{:S(2)}, u32[]{:S(2)}) collective-permute-start(bf16[1024,768]{1,0:T(8,128)(2,1)S(1)} %fusion.2), channel_id=1, source_target_pairs={{0,2},{1,3},{2,0},{3,1},{4,6},{5,7},{6,4},{7,5},{8,10},{9,11},{10,... | collective-permute-start | bytes 4718600 | tf_op jit(solution)/shard_map/ppermute | solution.py:17
  11.0 1.9 %exponential_reduce_fusion.4 = f32[1024]{0:T(1024)S(1)} fusion(bf16[1024,768]{1,0:T(8,128)(2,1)S(1)} %fusion.2), kind=kOutput, calls=%fused_computation.4 | convolution fusion | flops 1613757440 | bytes 1576960 | tf_op jit(solution)/shard_map/dot_general | solution.py:31
  13.0 26.8 %collective-permute-done.2 = bf16[1024,768]{1,0:T(8,128)(2,1)S(1)} collective-permute-done((bf16[1024,768]{1,0:T(8,128)(2,1)S(1)}, bf16[1024,768]{1,0:T(8,128)(2,1)S(1)}, u32[]{:S(2)}, u32[]{:S(2)}) %collective-permute-start.2) | collective-permute-done | bytes 1572896 | tf_op jit(solution)/shard_map/ppermute | solution.py:17
  39.8 1.9 %exponential_reduce_fusion.1 = f32[1024]{0:T(1024)S(1)} fusion(bf16[1024,768]{1,0:T(8,128)(2,1)S(1)} %fusion.2, bf16[1024,768]{1,0:T(8,128)(2,1)S(1)} %collective-permute-done.2), kind=kOutput, calls=%fused_computation.1 | convolution fusion | flops 1613757440 | bytes 3149824 | tf_op jit(solution)/shard_map/dot_general | solution.py:31
  41.7 33.1 %collective-permute-done.1 = bf16[1024,768]{1,0:T(8,128)(2,1)S(1)} collective-permute-done((bf16[1024,768]{1,0:T(8,128)(2,1)S(1)}, bf16[1024,768]{1,0:T(8,128)(2,1)S(1)}, u32[]{:S(2)}, u32[]{:S(2)}) %collective-permute-start.1) | collective-permute-done | bytes 1572896 | tf_op jit(solution)/shard_map/ppermute | solution.py:17
  74.8 1.9 %exponential_reduce_fusion.2 = f32[1024]{0:T(1024)S(1)} fusion(bf16[1024,768]{1,0:T(8,128)(2,1)S(1)} %fusion.2, bf16[1024,768]{1,0:T(8,128)(2,1)S(1)} %collective-permute-done.1), kind=kOutput, calls=%fused_computation.2 | convolution fusion | flops 1613757440 | bytes 3149824 | tf_op jit(solution)/shard_map/dot_general | solution.py:31
  76.8 0.4 collective-permute-done
  77.2 1.9 %exponential_reduce_fusion.3 = f32[1024]{0:T(1024)S(1)} fusion(bf16[1024,768]{1,0:T(8,128)(2,1)S(1)} %fusion.2, bf16[1024,768]{1,0:T(8,128)(2,1)S(1)} %collective-permute-done), kind=kOutput, calls=%fused_computation.3 | convolution fusion | flops 1613757440 | bytes 3149824 | tf_op jit(solution)/shard_map/dot_general | solution.py:31
  79.1 0.0 collective-permute-done.3
  79.1 1.9 %exponential_reduce_fusion = f32[1024]{0:T(1024)S(1)} fusion(bf16[1024,768]{1,0:T(8,128)(2,1)S(1)} %fusion.2, bf16[1024,768]{1,0:T(8,128)(2,1)S(1)} %collective-permute-done.3), kind=kOutput, calls=%fused_computation | convolution fusion | flops 1613757440 | bytes 3149824 | tf_op jit(solution)/shard_map/dot_general | solution.py:31
  81.1 0.6 fusion.3
  81.7 38.3 %psum.7 = f32[]{:T(128)} all-reduce(f32[]{:T(128)} %get-tuple-element.5), channel_id=1, replica_groups=mesh['dev'=32] {'dev'}, use_global_device_ids=true, to_apply=%region_7.0 | all-reduce | flops 1 | bytes 8 | tf_op jit(solution)/shard_map/psum | solution.py:53
  120.0 1.3 %multiply_divide_fusion = f32[1024]{0:T(1024)} fusion(f32[1024]{0:T(1024)S(1)} %get-tuple-element.6, f32[]{:T(128)} %psum.7), kind=kLoop, calls=%fused_computation.10 | loop fusion | flops 2048 | bytes 8196 | tf_op jit(solution)/shard_map/div | solution.py:54
  (1 shorter events, 0.0 us)
Async XLA Ops:
  0.0 1.9 %copy-start = (bf16[1024,768]{1,0:T(8,128)(2,1)S(1)}, bf16[1024,768]{1,0:T(8,128)(2,1)}, u32[]{:S(2)}) copy-start(bf16[1024,768]{1,0:T(8,128)(2,1)} %param.1) | copy-start | bytes 4718596
  2.4 37.4 %collective-permute-start.2 = (bf16[1024,768]{1,0:T(8,128)(2,1)S(1)}, bf16[1024,768]{1,0:T(8,128)(2,1)S(1)}, u32[]{:S(2)}, u32[]{:S(2)}) collective-permute-start(bf16[1024,768]{1,0:T(8,128)(2,1)S(1)} %fusion.2), channel_id=1, source_target_pairs={{0,4},{1,5},{2,6},{3,7},{4,0},{5,1},{6,2},{7,3},{8,12},{9,13},{10,... | collective-permute-start | bytes 4718600 | tf_op jit(solution)/shard_map/ppermute | solution.py:17
  5.4 69.4 %collective-permute-start.1 = (bf16[1024,768]{1,0:T(8,128)(2,1)S(1)}, bf16[1024,768]{1,0:T(8,128)(2,1)S(1)}, u32[]{:S(2)}, u32[]{:S(2)}) collective-permute-start(bf16[1024,768]{1,0:T(8,128)(2,1)S(1)} %fusion.2), channel_id=1, source_target_pairs={{0,8},{1,9},{2,10},{3,11},{4,12},{5,13},{6,14},{7,15},{8,0},{9,1},... | collective-permute-start | bytes 4718600 | tf_op jit(solution)/shard_map/ppermute | solution.py:17
  7.0 70.2 %collective-permute-start = (bf16[1024,768]{1,0:T(8,128)(2,1)S(1)}, bf16[1024,768]{1,0:T(8,128)(2,1)S(1)}, u32[]{:S(2)}, u32[]{:S(2)}) collective-permute-start(bf16[1024,768]{1,0:T(8,128)(2,1)S(1)} %fusion.2), channel_id=1, source_target_pairs={{0,16},{1,17},{2,18},{3,19},{4,20},{5,21},{6,22},{7,23},{8,24},{9,... | collective-permute-start | bytes 4718600 | tf_op jit(solution)/shard_map/ppermute | solution.py:17
  9.6 69.6 %collective-permute-start.3 = (bf16[1024,768]{1,0:T(8,128)(2,1)S(1)}, bf16[1024,768]{1,0:T(8,128)(2,1)S(1)}, u32[]{:S(2)}, u32[]{:S(2)}) collective-permute-start(bf16[1024,768]{1,0:T(8,128)(2,1)S(1)} %fusion.2), channel_id=1, source_target_pairs={{0,2},{1,3},{2,0},{3,1},{4,6},{5,7},{6,4},{7,5},{8,10},{9,11},{10,... | collective-permute-start | bytes 4718600 | tf_op jit(solution)/shard_map/ppermute | solution.py:17
where the time goes:
time: 122 us; the launch traced here: 121 us
  waiting for transfers between devices  60.3 us (49%)
  blocking collectives  38.3 us (31%)
  matrix products  9.62 us (8%)
  starting transfers between devices  8.69 us (7%)
  other arithmetic  4.23 us (3%)
    ppermute x4, waiting for transfers between devices, swapped(): return lax.ppermute(value, axis, pairs)  60.3 us
    psum x1, blocking collectives, shards(): total = lax.psum(jnp.sum(weights), 'dev')  38.3 us
    dot_general x5, matrix products, kernel_tile(): lax.dot_general(left, right, (((1,), (1,)), ((), ())), preferred_element_...  9.62 us
    ppermute x4, starting transfers between devices, swapped(): return lax.ppermute(value, axis, pairs)  8.69 us
  transfers between devices with their start and end apart: 4, of which 3 were waited for; matrix products, arithmetic and copies ran while one was open for 6% of the time, Pallas kernels for 0%

commit v1 on v0

v1 whole, which is shorter than its diff:
```python
import functools
import math

import jax
import jax.numpy as jnp
from jax import lax
from jax.experimental import pallas as pl
from jax.experimental.pallas import tpu as pltpu
from jax.sharding import PartitionSpec as P

ROUNDS = 4
LANES = 128
sharpness = 10.0


def bit_of(me, stride):
    return (me // stride) % 2


def flipped(me, stride):
    return me + stride * (1 - 2 * bit_of(me, stride))


def partners(n, me):
    top = n // 2
    found = []
    for first, second, extra in ((top, top // 2, 0), (top // 4, top // 8, 1)):
        parity = bit_of(me, first) + bit_of(me, second)
        if extra:
            parity = parity + me % 2
        parity = parity % 2
        a, b = flipped(me, first), flipped(me, second)
        target = a + parity * (b - a)
        source = b + parity * (a - b)
        found.append((target, source))
    return found


def normalize(values):
    widened = values.astype(jnp.float32)
    scaled = (
        widened
        * lax.rsqrt(jnp.mean(widened * widened, axis=1, keepdims=True) + 1e-06)
        / math.sqrt(values.shape[1])
    )
    return scaled.astype(jnp.bfloat16)


def kernel(
    n,
    emb_ref,
    out_ref,
    raw,
    normed,
    held,
    acc,
    sums,
    back,
    part,
    parts,
    load_sem,
    send_sem,
    recv_sem,
    sums_send,
    sums_recv,
    part_send,
    part_recv,
):
    rows = normed.shape[0]
    chunks = rows // LANES
    me = lax.axis_index("dev")

    def piece(c):
        return pl.ds(pl.multiple_of(c * LANES, LANES), LANES)

    def load(c):
        return pltpu.make_async_copy(
            emb_ref.at[piece(c)], raw.at[piece(c)], load_sem.at[c]
        )

    for c in range(chunks):
        load(c).start()

    barrier = pltpu.get_barrier_semaphore()

    @pl.loop(1, n)
    def _(step):
        pl.semaphore_signal(
            barrier,
            inc=1,
            device_id=((me + step) % n,),
            device_id_type=pl.DeviceIdType.MESH,
        )

    routes = partners(n, me)
    acc[...] = jnp.zeros_like(acc)

    def block_copy(way, c):
        return pltpu.make_async_remote_copy(
            src_ref=normed.at[piece(c)],
            dst_ref=held.at[way, piece(c)],
            send_sem=send_sem.at[way, c],
            recv_sem=recv_sem.at[way, c],
            device_id=(routes[way][0],),
            device_id_type=pl.DeviceIdType.MESH,
        )

    def sums_copy(way):
        return pltpu.make_async_remote_copy(
            src_ref=sums.at[way],
            dst_ref=back.at[way],
            send_sem=sums_send.at[way],
            recv_sem=sums_recv.at[way],
            device_id=(routes[way][1],),
            device_id_type=pl.DeviceIdType.MESH,
        )

    def prepare(c):
        load(c).wait()
        normed[piece(c), :] = normalize(raw[piece(c), :])

    prepare(0)
    pl.semaphore_wait(barrier, n - 1)
    for way in range(2):
        block_copy(way, 0).start()

    @pl.loop(1, chunks)
    def _(c):
        prepare(c)
        for way in range(2):
            block_copy(way, c).start()

    def tile(block):
        similarity = lax.dot_general(
            block,
            normed[...],
            (((1,), (1,)), ((), ())),
            preferred_element_type=jnp.float32,
        )
        values = jnp.exp(sharpness * (similarity - 1.0))
        acc[...] += jnp.sum(values.reshape(LANES // 8, 8, rows), axis=0)
        return values

    @pl.loop(0, chunks)
    def _(c):
        tile(normed[piece(c), :])

    for way in (1, 0):

        @pl.loop(0, chunks)
        def _(c):
            block_copy(way, c).wait_recv()
            values = tile(held[way, piece(c), :])
            folded = values[:, :LANES]
            for t in range(1, chunks):
                folded = folded + values[:, t * LANES : (t + 1) * LANES]
            sums[way, pl.ds(c, 1), :] = jnp.sum(folded.T, axis=0, keepdims=True)

        sums_copy(way).start()

    own = jnp.concatenate(
        [
            jnp.sum(acc[:, t * LANES : (t + 1) * LANES], axis=0, keepdims=True)
            for t in range(chunks)
        ],
        axis=0,
    )
    for way in (1, 0):
        sums_copy(way).wait_recv()
    weights = 1.0 / (own + back[0] + back[1])
    part[...] = jnp.sum(weights, axis=0, keepdims=True)

    @pl.loop(1, n)
    def _(step):
        pltpu.make_async_remote_copy(
            src_ref=part,
            dst_ref=parts.at[step - 1],
            send_sem=part_send,
            recv_sem=part_recv,
            device_id=((me + step) % n,),
            device_id_type=pl.DeviceIdType.MESH,
        ).start()

    for way in range(2):
        sums_copy(way).wait_send()

        @pl.loop(0, chunks)
        def _(c):
            block_copy(way, c).wait_send()

    pltpu.make_async_copy(parts, parts, part_recv).wait()
    total = jnp.sum(jnp.sum(parts[...], axis=0) + part[...])
    out_ref[...] = weights * (n * rows) / total
    pltpu.make_async_copy(parts, parts, part_send).wait()


def shards(embeddings):
    n = lax.axis_size("dev")
    rows, width = embeddings.shape
    chunks = rows // LANES
    tiles = ROUNDS // 2 + 1
    out = pl.pallas_call(
        functools.partial(kernel, n),
        out_shape=jax.ShapeDtypeStruct((chunks, LANES), jnp.float32),
        in_specs=[pl.BlockSpec(memory_space=pl.ANY)],
        out_specs=pl.BlockSpec(memory_space=pltpu.VMEM),
        scratch_shapes=[
            pltpu.VMEM((rows, width), jnp.bfloat16),
            pltpu.VMEM((rows, width), jnp.bfloat16),
            pltpu.VMEM((2, rows, width), jnp.bfloat16),
            pltpu.VMEM((8, rows), jnp.float32),
            pltpu.VMEM((2, chunks, LANES), jnp.float32),
            pltpu.VMEM((2, chunks, LANES), jnp.float32),
            pltpu.VMEM((1, LANES), jnp.float32),
            pltpu.VMEM((n - 1, 1, LANES), jnp.float32),
            pltpu.SemaphoreType.DMA((chunks,)),
            pltpu.SemaphoreType.DMA((2, chunks)),
            pltpu.SemaphoreType.DMA((2, chunks)),
            pltpu.SemaphoreType.DMA((2,)),
            pltpu.SemaphoreType.DMA((2,)),
            pltpu.SemaphoreType.DMA,
            pltpu.SemaphoreType.DMA,
        ],
        compiler_params=pltpu.CompilerParams(
            collective_id=0, has_side_effects=True, vmem_limit_bytes=63 * 2**20
        ),
        cost_estimate=pl.CostEstimate(
            flops=2 * tiles * rows * rows * width,
            bytes_accessed=2 * rows * width,
            transcendentals=tiles * rows * rows,
        ),
        name="pair_sums",
    )(embeddings)
    return out.reshape(rows)


def solution(mesh):
    return jax.shard_map(
        shards,
        mesh=mesh,
        in_specs=(P("dev", None),),
        out_specs=P("dev"),
        check_vma=False,
    )
```

time: 122 us -> 52 us (0.43)
  waiting for transfers between devices: 60.3 us -> 0 us
  Pallas kernels: 0 us -> 50.5 us
  blocking collectives: 38.3 us -> 0 us
  matrix products: 9.62 us -> 0 us
  starting transfers between devices: 8.69 us -> 0 us
  other arithmetic: 4.23 us -> 0 us
  local copies, waits for them, and re-layouts: 0.01 us -> 1.28 us
    ppermute x4 -> x0, waiting for transfers between devices: 60.3 us -> none  [swapped(): return lax.ppermute(value, axis, pairs)]
    pallas_call x0 -> x1, Pallas kernels: none -> 50.5 us  [shards(): pl.pallas_call(functools.partial(kernel, n), out_shape=jax.ShapeDtypeStru...]
    psum x1 -> x0, blocking collectives: 38.3 us -> none  [shards(): total = lax.psum(jnp.sum(weights), 'dev')]
    dot_general x5 -> x0, matrix products: 9.62 us -> none  [kernel_tile(): lax.dot_general(left, right, (((1,), (1,)), ((), ())), preferred_element_...]
    ppermute x4 -> x0, starting transfers between devices: 8.69 us -> none  [swapped(): return lax.ppermute(value, axis, pairs)]
    reduce_sum x2 -> x0, other arithmetic: 2.51 us -> none  [the longest x1 1.9 us: normalize(): jnp.mean(widened * widened, axis=1, keepdims=True) + 1e-06]
    div x1 -> x0, other arithmetic: 1.29 us -> none  [shards(): return weights * (player_count * tile_rows) / total]
    unnamed x2 -> x1, local copies, waits for them, and re-layouts: 0.01 us -> 1.28 us
  transfers between devices with their start and end apart: 4 -> 0, of which waited for: 3 -> 0; matrix products, arithmetic and copies ran while one was open for 6% -> 0% of each run, Pallas kernels for 0% -> 0%
where the time goes in v1:
time: 52 us; the launch traced here: 51.8 us
  Pallas kernels  50.5 us (97%)
  local copies, waits for them, and re-layouts  1.28 us (2%)
    pallas_call x1, Pallas kernels, shards(): pl.pallas_call(functools.partial(kernel, n), out_shape=jax.ShapeDtypeStru...  50.5 us
    unnamed x1, local copies, waits for them, and re-layouts  1.28 us

profile of v1, /device:TPU:0, one launch (start us, length us, event | category | flops | bytes accessed | tf_op | source)
XLA Modules:
  0.0 51.8 jit_solution(8171055460684792440)
XLA Ops:
  0.0 50.5 %pair_sums.1 = f32[8,128]{1,0:T(8,128)} custom-call(bf16[1024,768]{1,0:T(8,128)(2,1)} %emb_ref.1), custom_call_target="tpu_custom_call" | custom-call | flops 4831838208 | bytes 1572864 | tf_op jit(solution)/shard_map/pair_sums/pallas_call | solution.py:202
  50.5 1.3 %copy.3 = f32[1024]{0:T(1024)} copy(f32[1024]{0:T(1024)} %bitcast.1) | data formatting | bytes 8192

commit v2 on v1

--- a/solution.py
+++ b/solution.py
@@ -10,6 +10,7 @@
 
 ROUNDS = 4
 LANES = 128
+DEPTH = (2, 4)
 sharpness = 10.0
 
 
@@ -121,14 +122,12 @@
 
     prepare(0)
     pl.semaphore_wait(barrier, n - 1)
-    for way in range(2):
-        block_copy(way, 0).start()
-
-    @pl.loop(1, chunks)
-    def _(c):
-        prepare(c)
+    for c in range(chunks):
+        if c:
+            prepare(c)
         for way in range(2):
-            block_copy(way, c).start()
+            if c < DEPTH[way]:
+                block_copy(way, c).start()
 
     def tile(block):
         similarity = lax.dot_general(
@@ -141,21 +140,27 @@
         acc[...] += jnp.sum(values.reshape(LANES // 8, 8, rows), axis=0)
         return values
 
+    def meet(way, c):
+        block_copy(way, c).wait_recv()
+        block_copy(way, c).wait_send()
+
+        @pl.when(c + DEPTH[way] < chunks)
+        def _():
+            block_copy(way, c + DEPTH[way]).start()
+
+        values = tile(held[way, piece(c), :])
+        folded = values[:, :LANES]
+        for t in range(1, chunks):
+            folded = folded + values[:, t * LANES : (t + 1) * LANES]
+        sums[way, pl.ds(c, 1), :] = jnp.sum(folded.T, axis=0, keepdims=True)
+
     @pl.loop(0, chunks)
     def _(c):
         tile(normed[piece(c), :])
+        meet(1, c)
+        meet(0, c)
 
     for way in (1, 0):
-
-        @pl.loop(0, chunks)
-        def _(c):
-            block_copy(way, c).wait_recv()
-            values = tile(held[way, piece(c), :])
-            folded = values[:, :LANES]
-            for t in range(1, chunks):
-                folded = folded + values[:, t * LANES : (t + 1) * LANES]
-            sums[way, pl.ds(c, 1), :] = jnp.sum(folded.T, axis=0, keepdims=True)
-
         sums_copy(way).start()
 
     own = jnp.concatenate(
@@ -183,10 +188,6 @@
 
     for way in range(2):
         sums_copy(way).wait_send()
-
-        @pl.loop(0, chunks)
-        def _(c):
-            block_copy(way, c).wait_send()
 
     pltpu.make_async_copy(parts, parts, part_recv).wait()
     total = jnp.sum(jnp.sum(parts[...], axis=0) + part[...])

time: 52 us -> 52.6 us (1.012)
  Pallas kernels: 50.5 us -> 51.1 us
    pallas_call x1, Pallas kernels: 50.5 us -> 51.1 us  [shards(): pl.pallas_call(functools.partial(kernel, n), out_shape=jax.ShapeDtypeStru...]
where the time goes in v2:
time: 52.6 us; the launch traced here: 52.4 us
  Pallas kernels  51.1 us (97%)
  local copies, waits for them, and re-layouts  1.28 us (2%)
    pallas_call x1, Pallas kernels, shards(): pl.pallas_call(functools.partial(kernel, n), out_shape=jax.ShapeDtypeStru...  51.1 us
    unnamed x1, local copies, waits for them, and re-layouts  1.28 us

profile of v2, /device:TPU:0, one launch (start us, length us, event | category | flops | bytes accessed | tf_op | source)
XLA Modules:
  0.0 52.4 jit_solution(6107933758379262326)
XLA Ops:
  0.0 51.1 %pair_sums.1 = f32[8,128]{1,0:T(8,128)} custom-call(bf16[1024,768]{1,0:T(8,128)(2,1)} %emb_ref.1), custom_call_target="tpu_custom_call" | custom-call | flops 4831838208 | bytes 1572864 | tf_op jit(solution)/shard_map/pair_sums/pallas_call | solution.py:203
  51.2 1.3 %copy.3 = f32[1024]{0:T(1024)} copy(f32[1024]{0:T(1024)} %bitcast.1) | data formatting | bytes 8192

commit v3 on v2

--- a/solution.py
+++ b/solution.py
@@ -10,7 +10,8 @@
 
 ROUNDS = 4
 LANES = 128
-DEPTH = (2, 4)
+DEPTH = (2, 3)
+CHUNK = 256
 sharpness = 10.0
 
 
@@ -53,6 +54,7 @@
     out_ref,
     raw,
     normed,
+    turned,
     held,
     acc,
     sums,
@@ -68,11 +70,11 @@
     part_recv,
 ):
     rows = normed.shape[0]
-    chunks = rows // LANES
+    chunks = rows // CHUNK
     me = lax.axis_index("dev")
 
     def piece(c):
-        return pl.ds(pl.multiple_of(c * LANES, LANES), LANES)
+        return pl.ds(pl.multiple_of(c * CHUNK, CHUNK), CHUNK)
 
     def load(c):
         return pltpu.make_async_copy(
@@ -119,6 +121,9 @@
     def prepare(c):
         load(c).wait()
         normed[piece(c), :] = normalize(raw[piece(c), :])
+
+    def turn(c):
+        turned[:, piece(c)] = normed[piece(c), :].T
 
     prepare(0)
     pl.semaphore_wait(barrier, n - 1)
@@ -129,16 +134,25 @@
             if c < DEPTH[way]:
                 block_copy(way, c).start()
 
-    def tile(block):
-        similarity = lax.dot_general(
-            block,
-            normed[...],
-            (((1,), (1,)), ((), ())),
-            preferred_element_type=jnp.float32,
-        )
-        values = jnp.exp(sharpness * (similarity - 1.0))
-        acc[...] += jnp.sum(values.reshape(LANES // 8, 8, rows), axis=0)
-        return values
+    for c in range(chunks):
+        turn(c)
+
+    def tile(block, fold):
+        folded = None
+        for t in range(chunks):
+            columns = slice(t * CHUNK, (t + 1) * CHUNK)
+            similarity = jnp.dot(
+                block, turned[:, columns], preferred_element_type=jnp.float32
+            )
+            values = jnp.exp(sharpness * (similarity - 1.0))
+            acc[:, columns] += jnp.sum(
+                values.reshape(CHUNK // 8, 8, CHUNK), axis=0
+            )
+            if fold:
+                for u in range(0, CHUNK, LANES):
+                    term = values[:, u : u + LANES]
+                    folded = term if folded is None else folded + term
+        return folded
 
     def meet(way, c):
         block_copy(way, c).wait_recv()
@@ -148,15 +162,16 @@
         def _():
             block_copy(way, c + DEPTH[way]).start()
 
-        values = tile(held[way, piece(c), :])
-        folded = values[:, :LANES]
-        for t in range(1, chunks):
-            folded = folded + values[:, t * LANES : (t + 1) * LANES]
-        sums[way, pl.ds(c, 1), :] = jnp.sum(folded.T, axis=0, keepdims=True)
+        folded = tile(held[way, piece(c), :], True)
+        for u in range(CHUNK // LANES):
+            turned_sums = folded[u * LANES : (u + 1) * LANES].T
+            sums[way, pl.ds(c * (CHUNK // LANES) + u, 1), :] = jnp.sum(
+                turned_sums, axis=0, keepdims=True
+            )
 
     @pl.loop(0, chunks)
     def _(c):
-        tile(normed[piece(c), :])
+        tile(normed[piece(c), :], False)
         meet(1, c)
         meet(0, c)
 
@@ -166,7 +181,7 @@
     own = jnp.concatenate(
         [
             jnp.sum(acc[:, t * LANES : (t + 1) * LANES], axis=0, keepdims=True)
-            for t in range(chunks)
+            for t in range(rows // LANES)
         ],
         axis=0,
     )
@@ -198,20 +213,22 @@
 def shards(embeddings):
     n = lax.axis_size("dev")
     rows, width = embeddings.shape
-    chunks = rows // LANES
+    chunks = rows // CHUNK
+    slabs = rows // LANES
     tiles = ROUNDS // 2 + 1
     out = pl.pallas_call(
         functools.partial(kernel, n),
-        out_shape=jax.ShapeDtypeStruct((chunks, LANES), jnp.float32),
+        out_shape=jax.ShapeDtypeStruct((slabs, LANES), jnp.float32),
         in_specs=[pl.BlockSpec(memory_space=pl.ANY)],
         out_specs=pl.BlockSpec(memory_space=pltpu.VMEM),
         scratch_shapes=[
             pltpu.VMEM((rows, width), jnp.bfloat16),
             pltpu.VMEM((rows, width), jnp.bfloat16),
+            pltpu.VMEM((width, rows), jnp.bfloat16),
             pltpu.VMEM((2, rows, width), jnp.bfloat16),
             pltpu.VMEM((8, rows), jnp.float32),
-            pltpu.VMEM((2, chunks, LANES), jnp.float32),
-            pltpu.VMEM((2, chunks, LANES), jnp.float32),
+            pltpu.VMEM((2, slabs, LANES), jnp.float32),
+            pltpu.VMEM((2, slabs, LANES), jnp.float32),
             pltpu.VMEM((1, LANES), jnp.float32),
             pltpu.VMEM((n - 1, 1, LANES), jnp.float32),
             pltpu.SemaphoreType.DMA((chunks,)),

time: 52.6 us -> 52.4 us (level)
  no operation moved by 1% of the time
where the time goes in v3:
time: 52.4 us; the launch traced here: 52.2 us
  Pallas kernels  50.9 us (97%)
  local copies, waits for them, and re-layouts  1.28 us (2%)
    pallas_call x1, Pallas kernels, shards(): pl.pallas_call(functools.partial(kernel, n), out_shape=jax.ShapeDtypeStru...  50.9 us
    unnamed x1, local copies, waits for them, and re-layouts  1.28 us

profile of v3, /device:TPU:0, one launch (start us, length us, event | category | flops | bytes accessed | tf_op | source)
XLA Modules:
  0.0 52.2 jit_solution(216517684742327212)
XLA Ops:
  0.0 50.9 %pair_sums.1 = f32[8,128]{1,0:T(8,128)} custom-call(bf16[1024,768]{1,0:T(8,128)(2,1)} %emb_ref.1), custom_call_target="tpu_custom_call" | custom-call | flops 4831838208 | bytes 1572864 | tf_op jit(solution)/shard_map/pair_sums/pallas_call | solution.py:219
  50.9 1.3 %copy.3 = f32[1024]{0:T(1024)} copy(f32[1024]{0:T(1024)} %bitcast.1) | data formatting | bytes 8192

commit v4 on v3

--- a/solution.py
+++ b/solution.py
@@ -60,7 +60,8 @@
     sums,
     back,
     part,
-    parts,
+    near_parts,
+    far_parts,
     load_sem,
     send_sem,
     recv_sem,
@@ -81,19 +82,29 @@
             emb_ref.at[piece(c)], raw.at[piece(c)], load_sem.at[c]
         )
 
+    near = n // 4
+    groups = ((near, near_parts), (4, far_parts))
+
+    def peer(peers, step):
+        if peers == near:
+            return me // near * near + (me % near + step) % near
+        return (me + step * near) % n
+
     for c in range(chunks):
         load(c).start()
 
     barrier = pltpu.get_barrier_semaphore()
 
-    @pl.loop(1, n)
-    def _(step):
-        pl.semaphore_signal(
-            barrier,
-            inc=1,
-            device_id=((me + step) % n,),
-            device_id_type=pl.DeviceIdType.MESH,
-        )
+    for peers, _ in groups:
+
+        @pl.loop(1, peers)
+        def _(step):
+            pl.semaphore_signal(
+                barrier,
+                inc=1,
+                device_id=(peer(peers, step),),
+                device_id_type=pl.DeviceIdType.MESH,
+            )
 
     routes = partners(n, me)
     acc[...] = jnp.zeros_like(acc)
@@ -126,7 +137,7 @@
         turned[:, piece(c)] = normed[piece(c), :].T
 
     prepare(0)
-    pl.semaphore_wait(barrier, n - 1)
+    pl.semaphore_wait(barrier, near + 2)
     for c in range(chunks):
         if c:
             prepare(c)
@@ -188,26 +199,31 @@
     for way in (1, 0):
         sums_copy(way).wait_recv()
     weights = 1.0 / (own + back[0] + back[1])
-    part[...] = jnp.sum(weights, axis=0, keepdims=True)
-
-    @pl.loop(1, n)
-    def _(step):
-        pltpu.make_async_remote_copy(
-            src_ref=part,
-            dst_ref=parts.at[step - 1],
-            send_sem=part_send,
-            recv_sem=part_recv,
-            device_id=((me + step) % n,),
-            device_id_type=pl.DeviceIdType.MESH,
-        ).start()
-
-    for way in range(2):
-        sums_copy(way).wait_send()
-
-    pltpu.make_async_copy(parts, parts, part_recv).wait()
-    total = jnp.sum(jnp.sum(parts[...], axis=0) + part[...])
+    part[0] = jnp.sum(weights, axis=0, keepdims=True)
+
+    for stage, (peers, parts) in enumerate(groups):
+
+        @pl.loop(1, peers)
+        def _(step):
+            pltpu.make_async_remote_copy(
+                src_ref=part.at[stage],
+                dst_ref=parts.at[step - 1],
+                send_sem=part_send.at[stage],
+                recv_sem=part_recv.at[stage],
+                device_id=(peer(peers, step),),
+                device_id_type=pl.DeviceIdType.MESH,
+            ).start()
+
+        if stage == 0:
+            for way in range(2):
+                sums_copy(way).wait_send()
+        pltpu.make_async_copy(parts, parts, part_recv.at[stage]).wait()
+        part[stage + 1] = part[stage] + jnp.sum(parts[...], axis=0)
+
+    total = jnp.sum(part[2], axis=1, keepdims=True)
     out_ref[...] = weights * (n * rows) / total
-    pltpu.make_async_copy(parts, parts, part_send).wait()
+    for stage, (peers, parts) in enumerate(groups):
+        pltpu.make_async_copy(parts, parts, part_send.at[stage]).wait()
 
 
 def shards(embeddings):
@@ -229,15 +245,16 @@
             pltpu.VMEM((8, rows), jnp.float32),
             pltpu.VMEM((2, slabs, LANES), jnp.float32),
             pltpu.VMEM((2, slabs, LANES), jnp.float32),
-            pltpu.VMEM((1, LANES), jnp.float32),
-            pltpu.VMEM((n - 1, 1, LANES), jnp.float32),
+            pltpu.VMEM((3, 1, LANES), jnp.float32),
+            pltpu.VMEM((n // 4 - 1, 1, LANES), jnp.float32),
+            pltpu.VMEM((3, 1, LANES), jnp.float32),
             pltpu.SemaphoreType.DMA((chunks,)),
             pltpu.SemaphoreType.DMA((2, chunks)),
             pltpu.SemaphoreType.DMA((2, chunks)),
             pltpu.SemaphoreType.DMA((2,)),
             pltpu.SemaphoreType.DMA((2,)),
-            pltpu.SemaphoreType.DMA,
-            pltpu.SemaphoreType.DMA,
+            pltpu.SemaphoreType.DMA((2,)),
+            pltpu.SemaphoreType.DMA((2,)),
         ],
         compiler_params=pltpu.CompilerParams(
             collective_id=0, has_side_effects=True, vmem_limit_bytes=63 * 2**20

time: 52.4 us -> 53.7 us (1.025)
  Pallas kernels: 50.9 us -> 52.3 us
    pallas_call x1, Pallas kernels: 50.9 us -> 52.3 us  [shards(): pl.pallas_call(functools.partial(kernel, n), out_shape=jax.ShapeDtypeStru...]
where the time goes in v4:
time: 53.7 us; the launch traced here: 53.6 us
  Pallas kernels  52.3 us (97%)
  local copies, waits for them, and re-layouts  1.28 us (2%)
    pallas_call x1, Pallas kernels, shards(): pl.pallas_call(functools.partial(kernel, n), out_shape=jax.ShapeDtypeStru...  52.3 us
    unnamed x1, local copies, waits for them, and re-layouts  1.28 us

profile of v4, /device:TPU:0, one launch (start us, length us, event | category | flops | bytes accessed | tf_op | source)
XLA Modules:
  0.0 53.6 jit_solution(17312151454533781988)
XLA Ops:
  0.0 52.3 %pair_sums.1 = f32[8,128]{1,0:T(8,128)} custom-call(bf16[1024,768]{1,0:T(8,128)(2,1)} %emb_ref.1), custom_call_target="tpu_custom_call" | custom-call | flops 4831838208 | bytes 1572864 | tf_op jit(solution)/shard_map/pair_sums/pallas_call | solution.py:235
  52.3 1.3 %copy.3 = f32[1024]{0:T(1024)} copy(f32[1024]{0:T(1024)} %bitcast.1) | data formatting | bytes 8192

commit v5 on v3

--- a/solution.py
+++ b/solution.py
@@ -10,7 +10,7 @@
 
 ROUNDS = 4
 LANES = 128
-DEPTH = (2, 3)
+DEPTH = (4, 1)
 CHUNK = 256
 sharpness = 10.0
 

time: 52.4 us -> 52.4 us (level)
  no operation moved by 1% of the time
where the time goes in v5:
time: 52.4 us; the launch traced here: 52.2 us
  Pallas kernels  50.9 us (97%)
  local copies, waits for them, and re-layouts  1.28 us (2%)
    pallas_call x1, Pallas kernels, shards(): pl.pallas_call(functools.partial(kernel, n), out_shape=jax.ShapeDtypeStru...  50.9 us
    unnamed x1, local copies, waits for them, and re-layouts  1.28 us

profile of v5, /device:TPU:0, one launch (start us, length us, event | category | flops | bytes accessed | tf_op | source)
XLA Modules:
  0.0 52.2 jit_solution(6320217042946434355)
XLA Ops:
  0.0 50.9 %pair_sums.1 = f32[8,128]{1,0:T(8,128)} custom-call(bf16[1024,768]{1,0:T(8,128)(2,1)} %emb_ref.1), custom_call_target="tpu_custom_call" | custom-call | flops 4831838208 | bytes 1572864 | tf_op jit(solution)/shard_map/pair_sums/pallas_call | solution.py:219
  50.9 1.3 %copy.3 = f32[1024]{0:T(1024)} copy(f32[1024]{0:T(1024)} %bitcast.1) | data formatting | bytes 8192

commit v6 on v5

--- a/solution.py
+++ b/solution.py
@@ -10,7 +10,6 @@
 
 ROUNDS = 4
 LANES = 128
-DEPTH = (4, 1)
 CHUNK = 256
 sharpness = 10.0
 
@@ -68,6 +67,7 @@
     sums_recv,
     part_send,
     part_recv,
+    known,
 ):
     rows = normed.shape[0]
     chunks = rows // CHUNK
@@ -81,19 +81,22 @@
             emb_ref.at[piece(c)], raw.at[piece(c)], load_sem.at[c]
         )
 
-    for c in range(chunks):
-        load(c).start()
+    levels = n.bit_length() - 1
+    flips = [flipped(me, 1 << level) - me for level in range(levels)]
+
+    def across(mask):
+        return me + sum(flips[level] for level in range(levels) if mask >> level & 1)
 
     barrier = pltpu.get_barrier_semaphore()
-
-    @pl.loop(1, n)
-    def _(step):
+    for level in range(levels):
         pl.semaphore_signal(
             barrier,
             inc=1,
-            device_id=((me + step) % n,),
-            device_id_type=pl.DeviceIdType.MESH,
-        )
+            device_id=(across(1 << level),),
+            device_id_type=pl.DeviceIdType.MESH,
+        )
+    for c in range(chunks):
+        load(c).start()
 
     routes = partners(n, me)
     acc[...] = jnp.zeros_like(acc)
@@ -126,13 +129,12 @@
         turned[:, piece(c)] = normed[piece(c), :].T
 
     prepare(0)
-    pl.semaphore_wait(barrier, n - 1)
+    pl.semaphore_wait(barrier, levels)
     for c in range(chunks):
         if c:
             prepare(c)
         for way in range(2):
-            if c < DEPTH[way]:
-                block_copy(way, c).start()
+            block_copy(way, c).start()
 
     for c in range(chunks):
         turn(c)
@@ -156,12 +158,6 @@
 
     def meet(way, c):
         block_copy(way, c).wait_recv()
-        block_copy(way, c).wait_send()
-
-        @pl.when(c + DEPTH[way] < chunks)
-        def _():
-            block_copy(way, c + DEPTH[way]).start()
-
         folded = tile(held[way, piece(c), :], True)
         for u in range(CHUNK // LANES):
             turned_sums = folded[u * LANES : (u + 1) * LANES].T
@@ -172,6 +168,18 @@
     @pl.loop(0, chunks)
     def _(c):
         tile(normed[piece(c), :], False)
+
+    for level in range(levels):
+        pl.semaphore_signal(
+            known.at[level],
+            inc=1,
+            device_id=(across(1 << level),),
+            device_id_type=pl.DeviceIdType.MESH,
+        )
+        pl.semaphore_wait(known.at[level], 1)
+
+    @pl.loop(0, chunks)
+    def _(c):
         meet(1, c)
         meet(0, c)
 
@@ -190,22 +198,25 @@
     weights = 1.0 / (own + back[0] + back[1])
     part[...] = jnp.sum(weights, axis=0, keepdims=True)
 
-    @pl.loop(1, n)
-    def _(step):
+    for mask in range(n - 1, 0, -1):
         pltpu.make_async_remote_copy(
             src_ref=part,
-            dst_ref=parts.at[step - 1],
+            dst_ref=parts.at[mask - 1],
             send_sem=part_send,
             recv_sem=part_recv,
-            device_id=((me + step) % n,),
+            device_id=(across(mask),),
             device_id_type=pl.DeviceIdType.MESH,
         ).start()
 
     for way in range(2):
         sums_copy(way).wait_send()
 
+        @pl.loop(0, chunks)
+        def _(c):
+            block_copy(way, c).wait_send()
+
     pltpu.make_async_copy(parts, parts, part_recv).wait()
-    total = jnp.sum(jnp.sum(parts[...], axis=0) + part[...])
+    total = jnp.sum(jnp.sum(parts[...], axis=0) + part[...], axis=1, keepdims=True)
     out_ref[...] = weights * (n * rows) / total
     pltpu.make_async_copy(parts, parts, part_send).wait()
 
@@ -238,6 +249,7 @@
             pltpu.SemaphoreType.DMA((2,)),
             pltpu.SemaphoreType.DMA,
             pltpu.SemaphoreType.DMA,
+            pltpu.SemaphoreType.REGULAR((n.bit_length() - 1,)),
         ],
         compiler_params=pltpu.CompilerParams(
             collective_id=0, has_side_effects=True, vmem_limit_bytes=63 * 2**20

time: 52.4 us -> 51.7 us (0.987)
  Pallas kernels: 50.9 us -> 50.2 us
    pallas_call x1, Pallas kernels: 50.9 us -> 50.2 us  [shards(): pl.pallas_call(functools.partial(kernel, n), out_shape=jax.ShapeDtypeStru...]
where the time goes in v6:
time: 51.7 us; the launch traced here: 51.5 us
  Pallas kernels  50.2 us (97%)
  local copies, waits for them, and re-layouts  1.28 us (2%)
    pallas_call x1, Pallas kernels, shards(): pl.pallas_call(functools.partial(kernel, n), out_shape=jax.ShapeDtypeStru...  50.2 us
    unnamed x1, local copies, waits for them, and re-layouts  1.28 us

profile of v6, /device:TPU:0, one launch (start us, length us, event | category | flops | bytes accessed | tf_op | source)
XLA Modules:
  0.0 51.5 jit_solution(3606862065836054322)
XLA Ops:
  0.0 50.2 %pair_sums.1 = f32[8,128]{1,0:T(8,128)} custom-call(bf16[1024,768]{1,0:T(8,128)(2,1)} %emb_ref.1), custom_call_target="tpu_custom_call" | custom-call | flops 4831838208 | bytes 1572864 | tf_op jit(solution)/shard_map/pair_sums/pallas_call | solution.py:230
  50.3 1.3 %copy.3 = f32[1024]{0:T(1024)} copy(f32[1024]{0:T(1024)} %bitcast.1) | data formatting | bytes 8192

commit v7 on v6

--- a/solution.py
+++ b/solution.py
@@ -68,6 +68,13 @@
     part_send,
     part_recv,
     known,
+    go,
+    base,
+    other,
+    given,
+    weights,
+    base_sem,
+    given_sem,
 ):
     rows = normed.shape[0]
     chunks = rows // CHUNK
@@ -99,6 +106,8 @@
         load(c).start()
 
     routes = partners(n, me)
+    early = (bit_of(me, n // 2) + bit_of(me, n // 4) + me % 2) % 2
+    turns = (n // 2, n // 4, 1)
     acc[...] = jnp.zeros_like(acc)
 
     def block_copy(way, c):
@@ -133,8 +142,11 @@
     for c in range(chunks):
         if c:
             prepare(c)
-        for way in range(2):
-            block_copy(way, c).start()
+        block_copy(1, c).start()
+
+        @pl.when(early == 1)
+        def _():
+            block_copy(0, c).start()
 
     for c in range(chunks):
         turn(c)
@@ -178,47 +190,113 @@
         )
         pl.semaphore_wait(known.at[level], 1)
 
+    @pl.when(early == 1)
+    def _():
+        for c in range(chunks - 1):
+            block_copy(0, c).wait_send()
+        pl.semaphore_signal(
+            go,
+            inc=1,
+            device_id=(across(1),),
+            device_id_type=pl.DeviceIdType.MESH,
+        )
+
+    @pl.when(early == 0)
+    def _():
+        @pl.loop(0, chunks - 1)
+        def _(c):
+            meet(0, c)
+
+        pl.semaphore_wait(go, 1)
+        for c in range(chunks):
+            block_copy(0, c).start()
+        meet(0, chunks - 1)
+        sums_copy(0).start()
+
     @pl.loop(0, chunks)
     def _(c):
         meet(1, c)
-        meet(0, c)
-
-    for way in (1, 0):
-        sums_copy(way).start()
-
-    own = jnp.concatenate(
-        [
-            jnp.sum(acc[:, t * LANES : (t + 1) * LANES], axis=0, keepdims=True)
-            for t in range(rows // LANES)
-        ],
-        axis=0,
-    )
-    for way in (1, 0):
-        sums_copy(way).wait_recv()
-    weights = 1.0 / (own + back[0] + back[1])
-    part[...] = jnp.sum(weights, axis=0, keepdims=True)
-
+
+    sums_copy(1).start()
+
+    def own():
+        return jnp.concatenate(
+            [
+                jnp.sum(acc[:, t * LANES : (t + 1) * LANES], axis=0, keepdims=True)
+                for t in range(rows // LANES)
+            ],
+            axis=0,
+        )
+
+    def plain_copy(src, dst, pair, device):
+        return pltpu.make_async_remote_copy(
+            src_ref=src,
+            dst_ref=dst,
+            send_sem=pair.at[0],
+            recv_sem=pair.at[1],
+            device_id=(device,),
+            device_id_type=pl.DeviceIdType.MESH,
+        )
+
+    base_copy = plain_copy(base, other, base_sem, routes[0][0])
+    given_copy = plain_copy(given, weights, given_sem, routes[0][1])
+
+    kinds = ([], [])
     for mask in range(n - 1, 0, -1):
-        pltpu.make_async_remote_copy(
-            src_ref=part,
-            dst_ref=parts.at[mask - 1],
-            send_sem=part_send,
-            recv_sem=part_recv,
-            device_id=(across(mask),),
-            device_id_type=pl.DeviceIdType.MESH,
-        ).start()
-
-    for way in range(2):
-        sums_copy(way).wait_send()
+        kinds[sum(1 for turn in turns if mask & turn) % 2].append(mask)
+    same = len(kinds[0])
+
+    sums_copy(1).wait_recv()
+
+    @pl.when(early == 0)
+    def _():
+        base[...] = own() + back[1]
+        base_copy.start()
+        given_copy.wait_recv()
+        pltpu.make_async_copy(parts, parts, part_recv).wait()
+        base_copy.wait_send()
+        sums_copy(0).wait_send()
+        for c in range(chunks):
+            block_copy(0, c).wait_send()
+
+    @pl.when(early == 1)
+    def _():
+        sums_copy(0).wait_recv()
+        base_copy.wait_recv()
 
         @pl.loop(0, chunks)
         def _(c):
-            block_copy(way, c).wait_send()
-
-    pltpu.make_async_copy(parts, parts, part_recv).wait()
-    total = jnp.sum(jnp.sum(parts[...], axis=0) + part[...], axis=1, keepdims=True)
-    out_ref[...] = weights * (n * rows) / total
-    pltpu.make_async_copy(parts, parts, part_send).wait()
+            meet(0, c)
+
+        theirs = 1.0 / (other[...] + sums[0])
+        mine = 1.0 / (own() + back[0] + back[1])
+        given[...] = theirs
+        weights[...] = mine
+        part[...] = jnp.sum(theirs + mine, axis=0, keepdims=True)
+        given_copy.start()
+        for kind in (1, 0):
+            for slot, mask in enumerate(kinds[kind]):
+                pltpu.make_async_remote_copy(
+                    src_ref=part,
+                    dst_ref=parts.at[slot],
+                    send_sem=part_send.at[kind],
+                    recv_sem=part_recv,
+                    device_id=(across(mask),),
+                    device_id_type=pl.DeviceIdType.MESH,
+                ).start()
+        parts[same] = part[...]
+        head = parts.at[pl.ds(0, same)]
+        pltpu.make_async_copy(head, head, part_recv).wait()
+        given_copy.wait_send()
+        block_copy(0, chunks - 1).wait_send()
+        pltpu.make_async_copy(head, head, part_send.at[0]).wait()
+        pltpu.make_async_copy(parts, parts, part_send.at[1]).wait()
+
+    sums_copy(1).wait_send()
+    for c in range(chunks):
+        block_copy(1, c).wait_send()
+    total = jnp.sum(jnp.sum(parts[...], axis=0), axis=1, keepdims=True)
+    out_ref[...] = weights[...] * (n * rows) / total
 
 
 def shards(embeddings):
@@ -241,15 +319,22 @@
             pltpu.VMEM((2, slabs, LANES), jnp.float32),
             pltpu.VMEM((2, slabs, LANES), jnp.float32),
             pltpu.VMEM((1, LANES), jnp.float32),
-            pltpu.VMEM((n - 1, 1, LANES), jnp.float32),
+            pltpu.VMEM((n // 2, 1, LANES), jnp.float32),
             pltpu.SemaphoreType.DMA((chunks,)),
             pltpu.SemaphoreType.DMA((2, chunks)),
             pltpu.SemaphoreType.DMA((2, chunks)),
             pltpu.SemaphoreType.DMA((2,)),
             pltpu.SemaphoreType.DMA((2,)),
-            pltpu.SemaphoreType.DMA,
+            pltpu.SemaphoreType.DMA((2,)),
             pltpu.SemaphoreType.DMA,
             pltpu.SemaphoreType.REGULAR((n.bit_length() - 1,)),
+            pltpu.SemaphoreType.REGULAR,
+            pltpu.VMEM((slabs, LANES), jnp.float32),
+            pltpu.VMEM((slabs, LANES), jnp.float32),
+            pltpu.VMEM((slabs, LANES), jnp.float32),
+            pltpu.VMEM((slabs, LANES), jnp.float32),
+            pltpu.SemaphoreType.DMA((2,)),
+            pltpu.SemaphoreType.DMA((2,)),
         ],
         compiler_params=pltpu.CompilerParams(
             collective_id=0, has_side_effects=True, vmem_limit_bytes=63 * 2**20

time: 51.7 us -> 50.8 us (0.983)
  Pallas kernels: 50.2 us -> 49.3 us
    pallas_call x1, Pallas kernels: 50.2 us -> 49.3 us  [shards(): pl.pallas_call(functools.partial(kernel, n), out_shape=jax.ShapeDtypeStru...]
where the time goes in v7:
time: 50.8 us; the launch traced here: 50.6 us
  Pallas kernels  49.3 us (97%)
  local copies, waits for them, and re-layouts  1.28 us (3%)
    pallas_call x1, Pallas kernels, shards(): pl.pallas_call(functools.partial(kernel, n), out_shape=jax.ShapeDtypeStru...  49.3 us
    unnamed x1, local copies, waits for them, and re-layouts  1.28 us

profile of v7, /device:TPU:0, one launch (start us, length us, event | category | flops | bytes accessed | tf_op | source)
XLA Modules:
  0.0 50.6 jit_solution(10757771846882751890)
XLA Ops:
  0.0 49.3 %pair_sums.1 = f32[8,128]{1,0:T(8,128)} custom-call(bf16[1024,768]{1,0:T(8,128)(2,1)} %emb_ref.1), custom_call_target="tpu_custom_call" | custom-call | flops 4831838208 | bytes 1572864 | tf_op jit(solution)/shard_map/pair_sums/pallas_call | solution.py:308
  49.3 1.3 %copy.3 = f32[1024]{0:T(1024)} copy(f32[1024]{0:T(1024)} %bitcast.1) | data formatting | bytes 8192

commit v8 on v7

--- a/solution.py
+++ b/solution.py
@@ -142,11 +142,12 @@
     for c in range(chunks):
         if c:
             prepare(c)
-        block_copy(1, c).start()
 
         @pl.when(early == 1)
         def _():
             block_copy(0, c).start()
+
+        block_copy(1, c).start()
 
     for c in range(chunks):
         turn(c)
@@ -192,7 +193,7 @@
 
     @pl.when(early == 1)
     def _():
-        for c in range(chunks - 1):
+        for c in range(chunks - 2):
             block_copy(0, c).wait_send()
         pl.semaphore_signal(
             go,
@@ -203,14 +204,14 @@
 
     @pl.when(early == 0)
     def _():
-        @pl.loop(0, chunks - 1)
-        def _(c):
-            meet(0, c)
-
         pl.semaphore_wait(go, 1)
         for c in range(chunks):
             block_copy(0, c).start()
-        meet(0, chunks - 1)
+
+        @pl.loop(0, chunks)
+        def _(c):
+            meet(0, c)
+
         sums_copy(0).start()
 
     @pl.loop(0, chunks)
@@ -288,7 +289,8 @@
         head = parts.at[pl.ds(0, same)]
         pltpu.make_async_copy(head, head, part_recv).wait()
         given_copy.wait_send()
-        block_copy(0, chunks - 1).wait_send()
+        for c in range(chunks - 2, chunks):
+            block_copy(0, c).wait_send()
         pltpu.make_async_copy(head, head, part_send.at[0]).wait()
         pltpu.make_async_copy(parts, parts, part_send.at[1]).wait()
 

time: 50.8 us -> 50.6 us (level)
  no operation moved by 1% of the time
where the time goes in v8:
time: 50.6 us; the launch traced here: 50.4 us
  Pallas kernels  49.1 us (97%)
  local copies, waits for them, and re-layouts  1.28 us (3%)
    pallas_call x1, Pallas kernels, shards(): pl.pallas_call(functools.partial(kernel, n), out_shape=jax.ShapeDtypeStru...  49.1 us
    unnamed x1, local copies, waits for them, and re-layouts  1.28 us

profile of v8, /device:TPU:0, one launch (start us, length us, event | category | flops | bytes accessed | tf_op | source)
XLA Modules:
  0.0 50.4 jit_solution(7752588409348603388)
XLA Ops:
  0.0 49.1 %pair_sums.1 = f32[8,128]{1,0:T(8,128)} custom-call(bf16[1024,768]{1,0:T(8,128)(2,1)} %emb_ref.1), custom_call_target="tpu_custom_call" | custom-call | flops 4831838208 | bytes 1572864 | tf_op jit(solution)/shard_map/pair_sums/pallas_call | solution.py:310
  49.1 1.3 %copy.3 = f32[1024]{0:T(1024)} copy(f32[1024]{0:T(1024)} %bitcast.1) | data formatting | bytes 8192

commit v9 on v8

--- a/solution.py
+++ b/solution.py
@@ -10,7 +10,8 @@
 
 ROUNDS = 4
 LANES = 128
-CHUNK = 256
+CHUNK = 128
+PART = 256
 sharpness = 10.0
 
 
@@ -154,17 +155,17 @@
 
     def tile(block, fold):
         folded = None
-        for t in range(chunks):
-            columns = slice(t * CHUNK, (t + 1) * CHUNK)
+        for t in range(rows // PART):
+            columns = slice(t * PART, (t + 1) * PART)
             similarity = jnp.dot(
                 block, turned[:, columns], preferred_element_type=jnp.float32
             )
             values = jnp.exp(sharpness * (similarity - 1.0))
             acc[:, columns] += jnp.sum(
-                values.reshape(CHUNK // 8, 8, CHUNK), axis=0
+                values.reshape(CHUNK // 8, 8, PART), axis=0
             )
             if fold:
-                for u in range(0, CHUNK, LANES):
+                for u in range(0, PART, LANES):
                     term = values[:, u : u + LANES]
                     folded = term if folded is None else folded + term
         return folded
@@ -193,7 +194,7 @@
 
     @pl.when(early == 1)
     def _():
-        for c in range(chunks - 2):
+        for c in range(chunks // 2):
             block_copy(0, c).wait_send()
         pl.semaphore_signal(
             go,
@@ -289,7 +290,7 @@
         head = parts.at[pl.ds(0, same)]
         pltpu.make_async_copy(head, head, part_recv).wait()
         given_copy.wait_send()
-        for c in range(chunks - 2, chunks):
+        for c in range(chunks // 2, chunks):
             block_copy(0, c).wait_send()
         pltpu.make_async_copy(head, head, part_send.at[0]).wait()
         pltpu.make_async_copy(parts, parts, part_send.at[1]).wait()

time: 50.6 us -> 52.7 us (1.042)
  Pallas kernels: 49.1 us -> 51.3 us
    pallas_call x1, Pallas kernels: 49.1 us -> 51.3 us  [shards(): pl.pallas_call(functools.partial(kernel, n), out_shape=jax.ShapeDtypeStru...]
where the time goes in v9:
time: 52.7 us; the launch traced here: 52.5 us
  Pallas kernels  51.3 us (97%)
  local copies, waits for them, and re-layouts  1.28 us (2%)
    pallas_call x1, Pallas kernels, shards(): pl.pallas_call(functools.partial(kernel, n), out_shape=jax.ShapeDtypeStru...  51.3 us
    unnamed x1, local copies, waits for them, and re-layouts  1.28 us

profile of v9, /device:TPU:0, one launch (start us, length us, event | category | flops | bytes accessed | tf_op | source)
XLA Modules:
  0.0 52.5 jit_solution(9923152541010062561)
XLA Ops:
  0.0 51.3 %pair_sums.1 = f32[8,128]{1,0:T(8,128)} custom-call(bf16[1024,768]{1,0:T(8,128)(2,1)} %emb_ref.1), custom_call_target="tpu_custom_call" | custom-call | flops 4831838208 | bytes 1572864 | tf_op jit(solution)/shard_map/pair_sums/pallas_call | solution.py:311
  51.3 1.3 %copy.3 = f32[1024]{0:T(1024)} copy(f32[1024]{0:T(1024)} %bitcast.1) | data formatting | bytes 8192

commit v10 on v8

--- a/solution.py
+++ b/solution.py
@@ -247,10 +247,9 @@
         kinds[sum(1 for turn in turns if mask & turn) % 2].append(mask)
     same = len(kinds[0])
 
-    sums_copy(1).wait_recv()
-
     @pl.when(early == 0)
     def _():
+        sums_copy(1).wait_recv()
         base[...] = own() + back[1]
         base_copy.start()
         given_copy.wait_recv()
@@ -262,13 +261,13 @@
 
     @pl.when(early == 1)
     def _():
-        sums_copy(0).wait_recv()
-        base_copy.wait_recv()
-
         @pl.loop(0, chunks)
         def _(c):
             meet(0, c)
 
+        for way in range(2):
+            sums_copy(way).wait_recv()
+        base_copy.wait_recv()
         theirs = 1.0 / (other[...] + sums[0])
         mine = 1.0 / (own() + back[0] + back[1])
         given[...] = theirs

time: 50.6 us -> 48.2 us (0.953)
  Pallas kernels: 49.1 us -> 46.7 us
    pallas_call x1, Pallas kernels: 49.1 us -> 46.7 us  [shards(): pl.pallas_call(functools.partial(kernel, n), out_shape=jax.ShapeDtypeStru...]
where the time goes in v10:
time: 48.2 us; the launch traced here: 48 us
  Pallas kernels  46.7 us (97%)
  local copies, waits for them, and re-layouts  1.28 us (3%)
    pallas_call x1, Pallas kernels, shards(): pl.pallas_call(functools.partial(kernel, n), out_shape=jax.ShapeDtypeStru...  46.7 us
    unnamed x1, local copies, waits for them, and re-layouts  1.28 us

profile of v10, /device:TPU:0, one launch (start us, length us, event | category | flops | bytes accessed | tf_op | source)
XLA Modules:
  0.0 48.0 jit_solution(1956405832211213360)
XLA Ops:
  0.0 46.7 %pair_sums.1 = f32[8,128]{1,0:T(8,128)} custom-call(bf16[1024,768]{1,0:T(8,128)(2,1)} %emb_ref.1), custom_call_target="tpu_custom_call" | custom-call | flops 4831838208 | bytes 1572864 | tf_op jit(solution)/shard_map/pair_sums/pallas_call | solution.py:309
  46.7 1.3 %copy.3 = f32[1024]{0:T(1024)} copy(f32[1024]{0:T(1024)} %bitcast.1) | data formatting | bytes 8192

commit v11 on v9

--- a/solution.py
+++ b/solution.py
@@ -248,10 +248,9 @@
         kinds[sum(1 for turn in turns if mask & turn) % 2].append(mask)
     same = len(kinds[0])
 
-    sums_copy(1).wait_recv()
-
     @pl.when(early == 0)
     def _():
+        sums_copy(1).wait_recv()
         base[...] = own() + back[1]
         base_copy.start()
         given_copy.wait_recv()
@@ -263,13 +262,13 @@
 
     @pl.when(early == 1)
     def _():
-        sums_copy(0).wait_recv()
-        base_copy.wait_recv()
-
         @pl.loop(0, chunks)
         def _(c):
             meet(0, c)
 
+        for way in range(2):
+            sums_copy(way).wait_recv()
+        base_copy.wait_recv()
         theirs = 1.0 / (other[...] + sums[0])
         mine = 1.0 / (own() + back[0] + back[1])
         given[...] = theirs

time: 52.7 us -> 48.7 us (0.924)
  Pallas kernels: 51.3 us -> 47.3 us
    pallas_call x1, Pallas kernels: 51.3 us -> 47.3 us  [shards(): pl.pallas_call(functools.partial(kernel, n), out_shape=jax.ShapeDtypeStru...]
where the time goes in v11:
time: 48.7 us; the launch traced here: 48.6 us
  Pallas kernels  47.3 us (97%)
  local copies, waits for them, and re-layouts  1.28 us (3%)
    pallas_call x1, Pallas kernels, shards(): pl.pallas_call(functools.partial(kernel, n), out_shape=jax.ShapeDtypeStru...  47.3 us
    unnamed x1, local copies, waits for them, and re-layouts  1.28 us

profile of v11, /device:TPU:0, one launch (start us, length us, event | category | flops | bytes accessed | tf_op | source)
XLA Modules:
  0.0 48.6 jit_solution(316373037869930451)
XLA Ops:
  0.0 47.3 %pair_sums.1 = f32[8,128]{1,0:T(8,128)} custom-call(bf16[1024,768]{1,0:T(8,128)(2,1)} %emb_ref.1), custom_call_target="tpu_custom_call" | custom-call | flops 4831838208 | bytes 1572864 | tf_op jit(solution)/shard_map/pair_sums/pallas_call | solution.py:310
  47.3 1.3 %copy.3 = f32[1024]{0:T(1024)} copy(f32[1024]{0:T(1024)} %bitcast.1) | data formatting | bytes 8192

commit v12 on v10

--- a/solution.py
+++ b/solution.py
@@ -193,7 +193,7 @@
 
     @pl.when(early == 1)
     def _():
-        for c in range(chunks - 2):
+        for c in range(chunks - 1):
             block_copy(0, c).wait_send()
         pl.semaphore_signal(
             go,
@@ -288,7 +288,7 @@
         head = parts.at[pl.ds(0, same)]
         pltpu.make_async_copy(head, head, part_recv).wait()
         given_copy.wait_send()
-        for c in range(chunks - 2, chunks):
+        for c in range(chunks - 1, chunks):
             block_copy(0, c).wait_send()
         pltpu.make_async_copy(head, head, part_send.at[0]).wait()
         pltpu.make_async_copy(parts, parts, part_send.at[1]).wait()

time: 48.2 us -> 48.2 us (level)
  no operation moved by 1% of the time
where the time goes in v12:
time: 48.2 us; the launch traced here: 48 us
  Pallas kernels  46.7 us (97%)
  local copies, waits for them, and re-layouts  1.28 us (3%)
    pallas_call x1, Pallas kernels, shards(): pl.pallas_call(functools.partial(kernel, n), out_shape=jax.ShapeDtypeStru...  46.7 us
    unnamed x1, local copies, waits for them, and re-layouts  1.28 us

profile of v12, /device:TPU:0, one launch (start us, length us, event | category | flops | bytes accessed | tf_op | source)
XLA Modules:
  0.0 48.0 jit_solution(16007056708665925106)
XLA Ops:
  0.0 46.7 %pair_sums.1 = f32[8,128]{1,0:T(8,128)} custom-call(bf16[1024,768]{1,0:T(8,128)(2,1)} %emb_ref.1), custom_call_target="tpu_custom_call" | custom-call | flops 4831838208 | bytes 1572864 | tf_op jit(solution)/shard_map/pair_sums/pallas_call | solution.py:309
  46.7 1.3 %copy.3 = f32[1024]{0:T(1024)} copy(f32[1024]{0:T(1024)} %bitcast.1) | data formatting | bytes 8192
